TPU v7x, 256 devices: a whole 4x4x8 slice. The times are simulated.
256 devices in a mesh: depth: 4 (over y), row: 16 (over z, core), col: 4 (over x).
Axes of the slice: x: 4, y: 4, z: 8, core: 2. Of those that a mesh axis runs over, the one named last changes fastest.
Arguments:
- field: float32 [128, 2048, 2048], P('depth', 'row', 'col'), may hold values from 0.1 to 10
- view_order: int32 [4], replicated, may hold values from 0 to 3, each once
Outputs:
- image: float32 [4, 2048, 2048], P('depth', 'row', 'col')
Inputs may be any that keep to these rules, and one draw needn't show every extreme that they name: `view_order`: each brick index appears exactly once.
All inputs are finite; a program needn't handle non-finite values.
Results may differ from a plain program's by a relative error of at most 0.0003.
Values sent between devices are 32-bit elements; how exact they have to be, the bound alone decides.
A program may use at most 192 MiB of HBM per device.

v0:
```python
import jax
import jax.numpy as jnp
from jax import lax
from jax.sharding import PartitionSpec as P


def with_halo(shard, sides, width):
    for axis, dim in sides:
        peers, length = (lax.axis_size(axis), shard.shape[dim])
        up = [(i, (i + 1) % peers) for i in range(peers)]
        down = [(j, i) for i, j in up]
        last = lax.slice_in_dim(shard, length - width, length, axis=dim)
        leading = lax.slice_in_dim(shard, 0, width, axis=dim)
        before = lax.ppermute(last, axis, up)
        after = lax.ppermute(leading, axis, down)
        shard = jnp.concatenate([before, shard, after], axis=dim)
    return shard


def render(padded, opacity_scale):
    depth_cells = padded.shape[0] - 4
    row_cells = padded.shape[1] - 4
    col_cells = padded.shape[2] - 4

    def offset_view(shift_z, shift_y, shift_x):
        return padded[
            2 + shift_z : 2 + shift_z + depth_cells,
            2 + shift_y : 2 + shift_y + row_cells,
            2 + shift_x : 2 + shift_x + col_cells,
        ]

    centre = offset_view(0, 0, 0)
    grad_z = (
        8.0 * (offset_view(1, 0, 0) - offset_view(-1, 0, 0))
        - (offset_view(2, 0, 0) - offset_view(-2, 0, 0))
    ) / 12.0
    grad_y = (
        8.0 * (offset_view(0, 1, 0) - offset_view(0, -1, 0))
        - (offset_view(0, 2, 0) - offset_view(0, -2, 0))
    ) / 12.0
    grad_x = (
        8.0 * (offset_view(0, 0, 1) - offset_view(0, 0, -1))
        - (offset_view(0, 0, 2) - offset_view(0, 0, -2))
    ) / 12.0
    shading = 0.3 + 0.7 * jnp.abs(0.48 * grad_z + 0.6 * grad_y + 0.64 * grad_x) / jnp.sqrt(
        grad_z * grad_z + grad_y * grad_y + grad_x * grad_x + 1.0
    )
    bright = centre / (1.0 + centre)
    tau = opacity_scale * 2.0 * bright
    inclusive = jnp.cumsum(tau, axis=0)
    weight = jnp.exp(-(inclusive - tau)) * (1.0 - jnp.exp(-tau)) * 2.0 * shading
    red_sum = jnp.sum(weight * bright, axis=0)
    green_sum = jnp.sum(weight / (1.0 + centre), axis=0)
    blue_sum = jnp.sum(weight * 4.0 * bright / (1.0 + centre), axis=0)
    through = jnp.exp(-inclusive[-1])
    return (jnp.stack([red_sum, green_sum, blue_sum]), through)


def per_device(field, view_order):
    depth_count = lax.axis_size("depth")
    opacity_scale = 1.5 / (field.shape[0] * depth_count)
    padded = with_halo(field, (("depth", 0), ("row", 1), ("col", 2)), 2)
    colors, through = render(padded, opacity_scale)
    partial_value = jnp.concatenate([colors, (1.0 - through)[None]], axis=0)
    all_through = lax.all_gather(through[None], "depth", axis=0, tiled=True)
    positions = jnp.arange(depth_count, dtype=jnp.int32)
    view_rank = jnp.sum(
        positions[None, :] * (view_order[None, :] == positions[:, None]).astype(jnp.int32), axis=1
    )
    in_front = view_rank[None, :] < view_rank[:, None]
    factor = jnp.prod(jnp.where(in_front[:, :, None, None], all_through[None], 1.0), axis=1)
    own_factor = lax.dynamic_index_in_dim(factor, lax.axis_index("depth"), 0, keepdims=True)
    return lax.psum_scatter(own_factor * partial_value, "depth", scatter_dimension=0, tiled=True)


def solution(mesh):
    in_specs = (P("depth", "row", "col"), P())
    out_specs = P("depth", "row", "col")
    return jax.shard_map(
        per_device, mesh=mesh, in_specs=in_specs, out_specs=out_specs, check_vma=False
    )
```

profile of v0, /device:TPU:2, one launch (start us, length us, event | category | flops | bytes accessed | tf_op | source)
XLA Modules:
  0.0 199.4 jit_solution(7851401753310228360)
XLA Ops:
  6.5 0.0 all-gather.2.cloned.1.call-start
  6.5 1.3 fusion.18
  7.8 1.7 collective-permute-start.1
  9.5 1.7 collective-permute-start
  11.2 11.7 %collective-permute-done.1 = f32[2,128,512]{2,1,0:T(8,128)S(1)} collective-permute-done((f32[2,128,512]{2,1,0:T(8,128)S(1)}, f32[2,128,512]{2,1,0:T(8,128)S(1)}, u32[]{:S(2)}, u32[]{:S(2)}) %collective-permute-start.1) | collective-permute-done | bytes 524320 | tf_op jit(solution)/shard_map/ppermute | solution.py:14
  22.9 0.9 constant_dynamic-update-slice_fusion.3
  23.7 7.5 %constant_dynamic-update-slice_fusion.1 = (f32[34,128,512]{2,1,0:T(8,128)S(1)}, f32[36,128,512]{2,1,0:T(8,128)S(1)}, f32[34,128,512]{2,1,0:T(8,128)}) fusion(f32[32,128,512]{2,1,0:T(8,128)} %param.2, f32[36,128,512]{2,1,0:T(8,128)S(1)} %get-tuple-element.24, f32[34,128,512]{2,1,0:T(8,128)} %get-tuple-element.23), kind=kLoop, calls=%fused_computation.42 | loop fusion | bytes 33554432
  31.2 0.0 collective-permute-done
  31.2 0.1 constant_dynamic-update-slice_fusion
  31.4 0.0 copy-start
  31.4 0.0 copy-start.1
  31.4 0.1 fusion.17
  31.5 4.5 %collective-permute-start.2 = (f32[36,2,512]{2,1,0:T(2,128)S(1)}, f32[36,2,512]{2,1,0:T(2,128)S(1)}, u32[]{:S(2)}, u32[]{:S(2)}) collective-permute-start(f32[36,2,512]{2,1,0:T(2,128)S(1)} %get-tuple-element.13), channel_id=1, source_target_pairs={{4,0},{8,4},{12,8},{16,12},{20,16},{24,20},{28,24},{32,28},{36,32}... | collective-permute-start | bytes 442376 | tf_op jit(solution)/shard_map/ppermute | solution.py:15
  36.0 0.0 collective-permute-start.3
  36.0 2.7 %collective-permute-done.2 = f32[36,2,512]{2,1,0:T(2,128)S(1)} collective-permute-done((f32[36,2,512]{2,1,0:T(2,128)S(1)}, f32[36,2,512]{2,1,0:T(2,128)S(1)}, u32[]{:S(2)}, u32[]{:S(2)}) %collective-permute-start.2) | collective-permute-done | bytes 147488 | tf_op jit(solution)/shard_map/ppermute | solution.py:15
  38.7 3.1 %collective-permute-done.3 = f32[36,2,512]{2,1,0:T(2,128)S(1)} collective-permute-done((f32[36,2,512]{2,1,0:T(2,128)S(1)}, f32[36,2,512]{2,1,0:T(2,128)S(1)}, u32[]{:S(2)}, u32[]{:S(2)}) %collective-permute-start.3) | collective-permute-done | bytes 147488 | tf_op jit(solution)/shard_map/ppermute | solution.py:14
  41.8 0.0 copy-done
  41.8 2.5 %pad_maximum_fusion.5 = (f32[36,132,2]{2,1,0:T(8,128)S(1)}, f32[36,132,2]{2,1,0:T(8,128)}) fusion(f32[36,2,512]{2,1,0:T(2,128)S(1)} %collective-permute-done.2, f32[36,128,512]{2,1,0:T(8,128)S(1)} %get-tuple-element.22, f32[36,2,512]{2,1,0:T(2,128)S(1)} %collective-permute-done.3), kind=kLoop, calls=%fused_computation.35 | loop fusion | flops 38016 | bytes 9808128 | tf_op jit(solution)/shard_map/slice | solution.py:13
  44.3 0.0 copy-done.1
  44.3 3.1 %copy.9 = f32[36,132,2]{1,2,0:T(2,128)S(1)} copy(f32[36,132,2]{2,1,0:T(8,128)} %get-tuple-element.11) | data formatting | bytes 76032 | tf_op jit(solution)/shard_map/slice | solution.py:12
  47.3 1.5 collective-permute-start.5
  48.9 1.3 copy.7
  50.2 0.8 collective-permute-start.4
  51.0 0.8 collective-permute-done.5
  51.7 2.3 %copy.10 = f32[36,132,2]{2,1,0:T(8,128)} copy(f32[36,132,2]{1,2,0:T(2,128)S(1)} %collective-permute-done.5) | data formatting | bytes 76032 | tf_op jit(solution)/shard_map/ppermute | solution.py:14
  54.0 0.8 collective-permute-done.4
  54.8 0.0 slice-start
  54.8 2.3 %copy.8 = f32[36,132,2]{2,1,0:T(8,128)} copy(f32[36,132,2]{1,2,0:T(2,128)S(1)} %collective-permute-done.4) | data formatting | bytes 76032 | tf_op jit(solution)/shard_map/ppermute | solution.py:15
  57.1 0.0 slice-start.1
  57.1 0.0 slice-start.2
  57.1 22.4 %pad_maximum_fusion = (f32[36,132,514]{2,1,0:T(8,128)}, f32[36,132,514]{2,1,0:T(8,128)}) fusion(f32[36,132,2]{2,1,0:T(8,128)} %copy.8, f32[36,2,512]{2,1,0:T(2,128)S(1)} %collective-permute-done.2, f32[36,128,512]{2,1,0:T(8,128)} %copy-done, f32[36,2,512]{2,1,0:T(2,128)S(1)} %collective-permute-done.3, f32[36,132,2]{2,1,0:T(8,128)} %copy.10), kind=kLoop, calls=%fused_computation | loop fusion | flops 14655168 | bytes 29348352 | tf_op jit(solution)/shard_map/concatenate | solution.py:16
  79.5 0.0 slice-done
  79.5 0.0 slice-done.1
  79.5 0.0 slice-done.2
  79.5 0.0 copy-start.2
  79.6 56.8 %multiply_reduce_fusion = (f32[128,512]{1,0:T(8,128)}, f32[128,512]{1,0:T(8,128)}, f32[128,512]{1,0:T(8,128)}, f32[32,128,512]{2,1,0:T(8,128)}) fusion(f32[32,128,512]{2,1,0:T(8,128)} %param.2, f32[36,132,514]{2,1,0:T(8,128)} %get-tuple-element.9, f32[36,132,514]{2,1,0:T(8,128)} %get-tuple-element.8, f32[36,128,512]{2,1,0:T(8,128)S(1)} %bitcast.6, ...), kind=kOutput, calls=%fused_computation.25 | output fusion | flops 180158464 | bytes 102793216 | tf_op jit(solution)/shard_map/jit(cumsum)/reduce_window_sum | solution.py:50
  136.4 1.7 fusion.15
  138.1 0.0 all-gather.2.cloned.1.call-update
  138.1 0.0 reduce-scatter.2.cloned.1.call-start
  138.2 0.0 copy-done.2
  138.2 0.1 select_reduce_fusion.1
  138.3 0.1 broadcast_compare_fusion
  138.4 23.6 %all-gather.2.cloned.1.call-done = f32[4,128,512]{2,1,0:T(8,128)} async-done(((f32[1,128,512]{2,1,0:T(8,128)}), f32[4,128,512]{2,1,0:T(8,128)}) %all-gather.2.cloned.1.call-update) | async-done | bytes 1048592 | tf_op jit(solution)/shard_map/all_gather | solution.py:65
  162.0 1.7 select_reduce_fusion
  163.7 2.2 %maximum_multiply_fusion = f32[4,128,512]{2,1,0:T(8,128)} fusion(f32[1,128,512]{2,1,0:T(8,128)S(1)} %get-tuple-element.15, f32[1,128,512]{2,1,0:T(8,128)} %bitcast.8, f32[1,128,512]{2,1,0:T(8,128)} %bitcast.9, f32[1,128,512]{2,1,0:T(8,128)} %bitcast.7, f32[128,512]{1,0:T(8,128)S(1)} %dynamic-slice_bitcast_fusion), kind=kLoop, calls=%fused_computation.36 | loop fusion | flops 1048576 | bytes 2359296 | tf_op jit(solution)/shard_map/mul | solution.py:73
  165.9 0.0 reduce-scatter.2.cloned.1.call-update
  166.0 26.6 %reduce-scatter.2.cloned.1.call-done = f32[1,128,512]{2,1,0:T(8,128)} async-done(((f32[4,128,512]{2,1,0:T(8,128)}), f32[1,128,512]{2,1,0:T(8,128)}) %reduce-scatter.2.cloned.1.call-update) | async-done | bytes 262160 | tf_op jit(solution)/shard_map/reduce_scatter | solution.py:73
  (2 shorter events, 0.0 us)
Async XLA Ops:
  6.5 155.4 %all-gather.2.cloned.1.call-start = ((), (), s32[]{:S(2)}) async-start(), calls=%async_computation.1 | async-start | bytes 1310720 | tf_op jit(solution)/shard_map/all_gather | solution.py:65
  7.8 15.0 %collective-permute-start.1 = (f32[2,128,512]{2,1,0:T(8,128)S(1)}, f32[2,128,512]{2,1,0:T(8,128)S(1)}, u32[]{:S(2)}, u32[]{:S(2)}) collective-permute-start(f32[2,128,512]{2,1,0:T(8,128)S(1)} %get-tuple-element.20), channel_id=1, source_target_pairs={{0,64},{64,128},{128,192},{192,0},{1,65},{65,129},{129,193},{193,1... | collective-permute-start | bytes 1572872 | tf_op jit(solution)/shard_map/ppermute | solution.py:14
  9.5 21.8 %collective-permute-start = (f32[2,128,512]{2,1,0:T(8,128)S(1)}, f32[2,128,512]{2,1,0:T(8,128)S(1)}, u32[]{:S(2)}, u32[]{:S(2)}) collective-permute-start(f32[2,128,512]{2,1,0:T(8,128)S(1)} %get-tuple-element.19), channel_id=1, source_target_pairs={{64,0},{128,64},{192,128},{0,192},{65,1},{129,65},{193,129},{1,193... | collective-permute-start | bytes 1572872 | tf_op jit(solution)/shard_map/ppermute | solution.py:15
  31.4 10.4 %copy-start = (f32[36,128,512]{2,1,0:T(8,128)}, f32[36,128,512]{2,1,0:T(8,128)S(1)}, u32[]{:S(2)}) copy-start(f32[36,128,512]{2,1,0:T(8,128)S(1)} %get-tuple-element.22) | copy-start | bytes 28311556
  31.4 12.9 %copy-start.1 = (f32[34,128,512]{2,1,0:T(8,128)}, f32[34,128,512]{2,1,0:T(8,128)S(1)}, u32[]{:S(2)}) copy-start(f32[34,128,512]{2,1,0:T(8,128)S(1)} %get-tuple-element.21) | copy-start | bytes 26738692
  31.5 7.2 %collective-permute-start.2 = (f32[36,2,512]{2,1,0:T(2,128)S(1)}, f32[36,2,512]{2,1,0:T(2,128)S(1)}, u32[]{:S(2)}, u32[]{:S(2)}) collective-permute-start(f32[36,2,512]{2,1,0:T(2,128)S(1)} %get-tuple-element.13), channel_id=1, source_target_pairs={{4,0},{8,4},{12,8},{16,12},{20,16},{24,20},{28,24},{32,28},{36,32}... | collective-permute-start | bytes 442376 | tf_op jit(solution)/shard_map/ppermute | solution.py:15
  36.0 5.8 %collective-permute-start.3 = (f32[36,2,512]{2,1,0:T(2,128)S(1)}, f32[36,2,512]{2,1,0:T(2,128)S(1)}, u32[]{:S(2)}, u32[]{:S(2)}) collective-permute-start(f32[36,2,512]{2,1,0:T(2,128)S(1)} %get-tuple-element.12), channel_id=1, source_target_pairs={{0,4},{4,8},{8,12},{12,16},{16,20},{20,24},{24,28},{28,32},{32,36}... | collective-permute-start | bytes 442376 | tf_op jit(solution)/shard_map/ppermute | solution.py:14
  47.3 4.4 %collective-permute-start.5 = (f32[36,132,2]{1,2,0:T(2,128)S(1)}, f32[36,132,2]{1,2,0:T(2,128)S(1)}, u32[]{:S(2)}, u32[]{:S(2)}) collective-permute-start(f32[36,132,2]{1,2,0:T(2,128)S(1)} %copy.9), channel_id=1, source_target_pairs={{0,1},{1,2},{2,3},{3,0},{4,5},{5,6},{6,7},{7,4},{8,9},{9,10},{10,1... | collective-permute-start | bytes 114056 | tf_op jit(solution)/shard_map/ppermute | solution.py:14
  50.2 4.6 %collective-permute-start.4 = (f32[36,132,2]{1,2,0:T(2,128)S(1)}, f32[36,132,2]{1,2,0:T(2,128)S(1)}, u32[]{:S(2)}, u32[]{:S(2)}) collective-permute-start(f32[36,132,2]{1,2,0:T(2,128)S(1)} %copy.7), channel_id=1, source_target_pairs={{1,0},{2,1},{3,2},{0,3},{5,4},{6,5},{7,6},{4,7},{9,8},{10,9},{11,1... | collective-permute-start | bytes 114056 | tf_op jit(solution)/shard_map/ppermute | solution.py:15
  54.8 24.7 %slice-start = ((s8[9437184]{0:T(1024)(128)(4,1)}), s8[1048576]{0:T(1024)(128)(4,1)S(1)}, s32[]{:S(2)}) async-start(s8[9437184]{0:T(1024)(128)(4,1)} %bitcast.5), calls=%async_computation.3 | async-start | bytes 2097152
  57.1 22.4 %slice-start.1 = ((s8[9437184]{0:T(1024)(128)(4,1)}), s8[4194304]{0:T(1024)(128)(4,1)S(1)}, s32[]{:S(2)}) async-start(s8[9437184]{0:T(1024)(128)(4,1)} %bitcast.5), calls=%async_computation.4 | async-start | bytes 8388608
  57.1 22.4 %slice-start.2 = ((s8[9437184]{0:T(1024)(128)(4,1)}), s8[4194304]{0:T(1024)(128)(4,1)S(1)}, s32[]{:S(2)}) async-start(s8[9437184]{0:T(1024)(128)(4,1)} %bitcast.5), calls=%async_computation.5 | async-start | bytes 8388608
  79.5 58.6 %copy-start.2 = (s32[4]{0:T(128)S(1)}, s32[4]{0:T(128)}, u32[]{:S(2)}) copy-start(s32[4]{0:T(128)} %param.3) | copy-start | bytes 52
  138.1 54.4 %reduce-scatter.2.cloned.1.call-start = ((), (), s32[]{:S(2)}) async-start(), calls=%async_computation.2 | async-start | bytes 1310720 | tf_op jit(solution)/shard_map/reduce_scatter | solution.py:73
Sparse Core Ops, SparseCore 0:
  138.2 23.6 all-gather.1
  166.1 26.4 reduce-scatter.1
where the time goes:
time: 200 us; the launch traced here: 199 us
  other arithmetic  87.5 us (44%)
  waiting for transfers between devices  69.2 us (35%)
  local copies, waits for them, and re-layouts  19 us (10%)
  between operations  13.5 us (7%)
  starting transfers between devices  10.2 us (5%)
    another operation x1, other arithmetic, render(): inclusive = jnp.cumsum(tau, axis=0)  56.8 us
    reduce_scatter x1, waiting for transfers between devices, per_device(): lax.psum_scatter(own_factor * partial_value, 'depth', scatter_dimension=0...  26.6 us
    all_gather x1, waiting for transfers between devices, per_device(): all_through = lax.all_gather(through[None], 'depth', axis=0, tiled=True)  23.6 us
    concatenate x1, other arithmetic, with_halo(): shard = jnp.concatenate([before, shard, after], axis=dim)  22.4 us
    ppermute x3, waiting for transfers between devices, with_halo(): before = lax.ppermute(last, axis, up)  15.6 us
    unnamed x14, local copies, waits for them, and re-layouts  8.41 us
    ppermute x3, starting transfers between devices, with_halo(): after = lax.ppermute(leading, axis, down)  6.93 us
  transfers between devices with their start and end apart: 8, of which 7 were waited for; matrix products, arithmetic and copies ran while one was open for 6% of the time, Pallas kernels for 0%

commit v1 on v0

v1 whole, which is shorter than its diff:
```python
import math

import jax
import jax.numpy as jnp
from jax import lax
from jax.experimental import pallas as pl
from jax.experimental.pallas import tpu as pltpu
from jax.sharding import PartitionSpec as P

MESH = pl.DeviceIdType.MESH
CZ, NY, NX = 32, 128, 512
NB = 4
GROUPS = 4
STEP = 4
TILES = ((1, 2), (0, 3))
KEXP = -1.5 * 2.0 / 128.0
BIAS = 0.3 / 0.448
SCALE = 2.0 * 0.448


def kernel(vo_ref, f_ref, o_ref, buf, xs, xr, stage, recv, fin, fbuf,
           ld, zss, zrs, yss, yrs, xss, xrs, ass, ars, fss, frs):
    d, r, c = lax.axis_index("depth"), lax.axis_index("row"), lax.axis_index("col")
    brick = lambda k: (lax.rem(d + k, NB), r, c)
    row_to = (lax.rem(r + 1, 16), lax.rem(r + 15, 16))
    col_to = (lax.rem(c + 1, 4), lax.rem(c + 3, 4))
    lane = lax.broadcasted_iota(jnp.int32, (8, 128), 1)

    barrier = pltpu.get_barrier_semaphore()
    others = [brick(1), brick(2), brick(3), (d, row_to[0], c), (d, row_to[1], c),
              (d, r, col_to[0]), (d, r, col_to[1])]
    for dev in others:
        pl.semaphore_signal(barrier, inc=1, device_id=dev, device_id_type=MESH)

    def load(t, g):
        return pltpu.make_async_copy(
            f_ref.at[:, pl.ds(32 * g, 32), pl.ds(128 * t, 128)],
            buf.at[pl.ds(2, CZ), t, pl.ds(8 + 32 * g, 32), :], ld.at[t, g])

    def zhalo(p, i, side, n):
        t, g = TILES[p][n], lax.rem(i + 1, GROUPS)
        src, dst, k = ((CZ - 2, 0, 1), (0, CZ + 2, 3))[side]
        return pltpu.make_async_remote_copy(
            f_ref.at[pl.ds(src, 2), pl.ds(32 * g, 32), pl.ds(128 * t, 128)],
            buf.at[pl.ds(dst, 2), t, pl.ds(8 + 32 * g, 32), :],
            zss.at[p, i, side, n], zrs.at[p, i, side, n],
            device_id=brick(k), device_id_type=MESH)

    def yhalo(t, side):
        src, dst = ((NY - 8, 0), (0, NY + 8))[side]
        return pltpu.make_async_remote_copy(
            f_ref.at[:, pl.ds(src, 8), pl.ds(128 * t, 128)],
            buf.at[pl.ds(2, CZ), t, pl.ds(dst, 8), :],
            yss.at[t, side], yrs.at[t, side],
            device_id=(d, row_to[side], c), device_id_type=MESH)

    def xhalo(side):
        return pltpu.make_async_remote_copy(
            xs, xr.at[side], xss.at[side], xrs.at[side],
            device_id=(d, r, col_to[side]), device_id_type=MESH)

    def part(j, k):
        return pltpu.make_async_remote_copy(
            stage.at[j, lax.rem(d + k, NB)], recv.at[j, k - 1],
            ass.at[j, k - 1], ars.at[j, k - 1],
            device_id=brick(k), device_id_type=MESH)

    def final(j, k, owner):
        p, g = j // GROUPS, lax.rem(j + 1, GROUPS)
        return pltpu.make_async_remote_copy(
            fin.at[j, lax.rem(d + k, NB)],
            fbuf.at[pl.ds(2 * p, 2), pl.ds(32 * g + 8 * owner, 8), :],
            fss.at[j, k - 1], frs.at[j, k - 1],
            device_id=brick(k), device_id_type=MESH)

    for t in (0, 3, 1, 2):
        for g in range(GROUPS):
            load(t, g).start()
    pl.semaphore_wait(barrier, len(others))

    for p in range(2):
        @pl.loop(0, GROUPS)
        def _(i):
            for side in range(2):
                for n in range(2):
                    zhalo(p, i, side, n).start()
    for side in (1, 0):
        for t in (1, 2, 0, 3):
            yhalo(t, side).start()

    for t in (0, 3):
        for g in range(GROUPS):
            load(t, g).wait()

    @pl.loop(0, NY // 8)
    def _(t):
        rows = pl.ds(pl.multiple_of(8 + 8 * t, 8), 8)
        left = [buf[2 + z, 0, rows, :] for z in range(CZ)]
        right = [buf[2 + z, 3, rows, :] for z in range(CZ)]
        w = 2
        while len(left) > 1:
            left = [jnp.where(lane < w, a, pltpu.roll(b, w, 1)) for a, b in zip(left[::2], left[1::2])]
            right = [jnp.where(lane >= 128 - w, b, pltpu.roll(a, 128 - w, 1)) for a, b in zip(right[::2], right[1::2])]
            w *= 2
        xs[pl.ds(pl.multiple_of(8 * t, 8), 8), :] = jnp.where(lane < 64, left[0], right[0])

    for side in range(2):
        xhalo(side).start()
    for t in (1, 2):
        for g in range(GROUPS):
            load(t, g).wait()

    def strip(p, j, g, q):
        row = pl.multiple_of(8 + 32 * g + 8 * q, 8)
        rows = pl.ds(row, 8)
        tiles = TILES[p]
        edge_rows = pl.ds(pl.multiple_of(32 * g + 8 * q, 8), 8)
        if p == 1:
            from_left, from_right = xr[0, edge_rows, :], xr[1, edge_rows, :]

        def body(zz, carry):
            z0 = zz * STEP
            state = list(carry)
            col = {t: [buf[z0 + m, t, rows, :] for m in range(STEP + 4)] for t in tiles}
            for m in range(STEP):
                z = z0 + m
                for n, t in enumerate(tiles):
                    energy, wsum, rsum, bsum = state[4 * n:4 * n + 4]
                    s = col[t][m + 2]
                    gz = 8.0 * (col[t][m + 3] - col[t][m + 1]) - (col[t][m + 4] - col[t][m])
                    yv = lambda o: buf[z + 2, t, pl.ds(row + o, 8), :]
                    gy = 8.0 * (yv(1) - yv(-1)) - (yv(2) - yv(-2))
                    if t == 0:
                        prv = pltpu.roll(from_left, 62 - 2 * z, 1)
                    elif t - 1 in tiles:
                        prv = col[t - 1][m + 2]
                    else:
                        prv = buf[z + 2, t - 1, rows, :]
                    if t == 3:
                        nxt = pltpu.roll(from_right, lax.rem(128 - 2 * z, 128), 1)
                    elif t + 1 in tiles:
                        nxt = col[t + 1][m + 2]
                    else:
                        nxt = buf[z + 2, t + 1, rows, :]
                    xp1 = pltpu.roll(jnp.where(lane < 1, nxt, s), 127, 1)
                    xp2 = pltpu.roll(jnp.where(lane < 2, nxt, s), 126, 1)
                    xm1 = pltpu.roll(jnp.where(lane >= 127, prv, s), 1, 1)
                    xm2 = pltpu.roll(jnp.where(lane >= 126, prv, s), 2, 1)
                    gx = 8.0 * (xp1 - xm1) - (xp2 - xm2)
                    norm = (gz * gz + gy * gy) + (gx * gx + 144.0)
                    along = (0.75 * gz + 0.9375 * gy) + gx
                    shade = jnp.abs(along) * lax.rsqrt(norm) + BIAS
                    recip = pl.reciprocal(1.0 + s)
                    bright = 1.0 - recip
                    after = energy * jnp.exp(bright * KEXP)
                    weight = (energy - after) * shade
                    red = weight * bright
                    state[4 * n:4 * n + 4] = [after, wsum + weight, rsum + red, bsum + red * recip]
            return tuple(state)

        one, zero = jnp.ones((8, 128), jnp.float32), jnp.zeros((8, 128), jnp.float32)
        state = lax.fori_loop(0, CZ // STEP, body, (one, zero, zero, zero) * 2)
        for n in range(2):
            energy, wsum, rsum, bsum = state[4 * n:4 * n + 4]
            stage[j, q, 0 + n] = SCALE * rsum
            stage[j, q, 2 + n] = SCALE * (wsum - rsum)
            stage[j, q, 4 + n] = 4.0 * SCALE * bsum
            stage[j, q, 6 + n] = energy

    for p in range(2):
        if p == 1:
            for side in range(2):
                xhalo(side).wait()

        @pl.loop(0, GROUPS)
        def _(i):
            j, g = GROUPS * p + i, lax.rem(i + 1, GROUPS)
            for side in range(2):
                for n in range(2):
                    zhalo(p, i, side, n).wait()
            if p == 0:
                for side, at in ((1, 2), (0, 3)):
                    @pl.when(i == at)
                    def _():
                        for t in range(4):
                            yhalo(t, side).wait()

            @pl.loop(0, 4)
            def _(q):
                strip(p, j, g, q)

            for k in range(1, NB):
                part(j, k).start()

    ranks = []
    for k in range(NB):
        b = lax.rem(d + NB - k, NB)
        rank = jnp.int32(0)
        for pos in range(1, NB):
            rank = rank + jnp.where(vo_ref[pos] == b, jnp.int32(pos), jnp.int32(0))
        ranks.append(jnp.full((8, 128), rank, jnp.int32))
    ahead = [[None if e == k else ranks[e] < ranks[k] for e in range(NB)] for k in range(NB)]

    for p in range(2):
        @pl.loop(0, GROUPS)
        def _(i):
            j, g = GROUPS * p + i, lax.rem(i + 1, GROUPS)
            for k in range(1, NB):
                part(j, k).wait()
            for n in range(2):
                get = lambda k, ch: stage[j, d, 2 * ch + n] if k == 0 else recv[j, k - 1, 2 * ch + n]
                through = [get(k, 3) for k in range(NB)]
                total = [jnp.zeros((8, 128), jnp.float32)] * 4
                for k in range(NB):
                    factor = jnp.ones((8, 128), jnp.float32)
                    for e in range(NB):
                        if e != k:
                            factor = factor * jnp.where(ahead[k][e], through[e], 1.0)
                    for ch in range(3):
                        total[ch] = total[ch] + factor * get(k, ch)
                    total[3] = total[3] + factor * (1.0 - through[k])
                for ch in range(4):
                    fin[j, ch, n] = total[ch]
            for k in range(1, NB):
                final(j, k, d).start()
            fbuf[pl.ds(2 * p, 2), pl.ds(pl.multiple_of(32 * g + 8 * d, 8), 8), :] = fin[j, d]

    @pl.loop(0, 2 * GROUPS)
    def _(j):
        for k in range(1, NB):
            final(j, k, lax.rem(d + NB - k, NB)).wait()

    for p in range(2):
        for n in range(2):
            o_ref[0, :, pl.ds(128 * TILES[p][n], 128)] = fbuf[2 * p + n]


def per_device(field, view_order):
    dma = pltpu.SemaphoreType.DMA
    vmem = lambda *shape: pltpu.VMEM(shape, jnp.float32)
    return pl.pallas_call(
        kernel,
        out_shape=jax.ShapeDtypeStruct((1, NY, NX), jnp.float32),
        in_specs=[pl.BlockSpec(memory_space=pltpu.SMEM), pl.BlockSpec(memory_space=pl.ANY)],
        out_specs=pl.BlockSpec(memory_space=pltpu.VMEM),
        scratch_shapes=[
            vmem(CZ + 4, 4, NY + 16, 128),
            vmem(NY, 128), vmem(2, NY, 128),
            vmem(8, 4, 8, 8, 128), vmem(8, 3, 8, 8, 128),
            vmem(8, 4, 2, 8, 128), vmem(4, NY, 128),
            dma((4, 4)), dma((2, 4, 2, 2)), dma((2, 4, 2, 2)), dma((4, 2)), dma((4, 2)),
            dma((2,)), dma((2,)), dma((8, 3)), dma((8, 3)), dma((8, 3)), dma((8, 3)),
        ],
        compiler_params=pltpu.CompilerParams(
            collective_id=0, has_side_effects=True, vmem_limit_bytes=48 << 20),
    )(view_order, field)


def solution(mesh):
    return jax.shard_map(
        per_device, mesh=mesh, in_specs=(P("depth", "row", "col"), P()),
        out_specs=P("depth", "row", "col"), check_vma=False)
```

time: 200 us -> 61.1 us (0.31)
  other arithmetic: 87.5 us -> 0 us
  waiting for transfers between devices: 69.2 us -> 0 us
  Pallas kernels: 0 us -> 59.7 us
  local copies, waits for them, and re-layouts: 19 us -> 1.36 us
  between operations: 13.5 us -> 0.01 us
  starting transfers between devices: 10.2 us -> 0 us
    pallas_call x0 -> x1, Pallas kernels: none -> 59.7 us  [per_device(): pl.pallas_call(kernel, out_shape=jax.ShapeDtypeStruct((1, NY, NX), jnp.fl...]
    another operation x1 -> x0, other arithmetic: 56.8 us -> none  [render(): inclusive = jnp.cumsum(tau, axis=0)]
    reduce_scatter x1 -> x0, waiting for transfers between devices: 26.6 us -> none  [per_device(): lax.psum_scatter(own_factor * partial_value, 'depth', scatter_dimension=0...]
    all_gather x1 -> x0, waiting for transfers between devices: 23.6 us -> none  [per_device(): all_through = lax.all_gather(through[None], 'depth', axis=0, tiled=True)]
    concatenate x1 -> x0, other arithmetic: 22.4 us -> none  [with_halo(): shard = jnp.concatenate([before, shard, after], axis=dim)]
    ppermute x6 -> x0, waiting for transfers between devices: 19 us -> none  [the longest x3 15.6 us: with_halo(): before = lax.ppermute(last, axis, up)]
    ppermute x6 -> x0, starting transfers between devices: 10.1 us -> none  [the longest x3 6.93 us: with_halo(): after = lax.ppermute(leading, axis, down)]
    unnamed x14 -> x3, local copies, waits for them, and re-layouts: 8.41 us -> 1.36 us
  transfers between devices with their start and end apart: 8 -> 0, of which waited for: 7 -> 0; matrix products, arithmetic and copies ran while one was open for 6% -> 0% of each run, Pallas kernels for 0% -> 0%
where the time goes in v1:
time: 61.1 us; the launch traced here: 61 us
  Pallas kernels  59.7 us (98%)
  local copies, waits for them, and re-layouts  1.36 us (2%)
    pallas_call x1, Pallas kernels, per_device(): pl.pallas_call(kernel, out_shape=jax.ShapeDtypeStruct((1, NY, NX), jnp.fl...  59.7 us
    unnamed x3, local copies, waits for them, and re-layouts  1.36 us

profile of v1, /device:TPU:2, one launch (start us, length us, event | category | flops | bytes accessed | tf_op | source)
XLA Modules:
  0.0 61.0 jit_solution(3567605474554445164)
XLA Ops:
  0.0 0.0 copy-start
  0.0 0.7 %copy-done = s32[4]{0:T(128)S(1)} copy-done((s32[4]{0:T(128)S(1)}, s32[4]{0:T(128)}, u32[]{:S(2)}) %copy-start) | copy-done | bytes 40
  0.7 59.7 %shard_map.28 = f32[1,128,512]{2,1,0:T(8,128)S(1)} custom-call(s32[4]{0:T(128)S(1)} %copy-done, f32[32,128,512]{2,1,0:T(8,128)} %f_ref.1), custom_call_target="tpu_custom_call" | custom-call | tf_op jit(solution)/shard_map/pallas_call | solution.py:241
  60.3 0.7 %copy.4 = f32[1,128,512]{2,1,0:T(8,128)} copy(f32[1,128,512]{2,1,0:T(8,128)S(1)} %shard_map.28) | data formatting | bytes 524288
Async XLA Ops:
  0.0 0.7 %copy-start = (s32[4]{0:T(128)S(1)}, s32[4]{0:T(128)}, u32[]{:S(2)}) copy-start(s32[4]{0:T(128)} %vo_ref.1) | copy-start | bytes 52

commit v2 on v1

--- a/solution.py
+++ b/solution.py
@@ -11,9 +11,9 @@
 CZ, NY, NX = 32, 128, 512
 NB = 4
 GROUPS = 4
-STEP = 4
+STEP = 16
 TILES = ((1, 2), (0, 3))
-KEXP = -1.5 * 2.0 / 128.0
+KEXP = -1.5 * 2.0 / 128.0 * math.log2(math.e)
 BIAS = 0.3 / 0.448
 SCALE = 2.0 * 0.448
 
@@ -25,6 +25,7 @@
     row_to = (lax.rem(r + 1, 16), lax.rem(r + 15, 16))
     col_to = (lax.rem(c + 1, 4), lax.rem(c + 3, 4))
     lane = lax.broadcasted_iota(jnp.int32, (8, 128), 1)
+    pair = lane // 2
 
     barrier = pltpu.get_barrier_semaphore()
     others = [brick(1), brick(2), brick(3), (d, row_to[0], c), (d, row_to[1], c),
@@ -92,17 +93,15 @@
         for g in range(GROUPS):
             load(t, g).wait()
 
-    @pl.loop(0, NY // 8)
+    @pl.loop(0, NY // 8, unroll=2)
     def _(t):
         rows = pl.ds(pl.multiple_of(8 + 8 * t, 8), 8)
-        left = [buf[2 + z, 0, rows, :] for z in range(CZ)]
-        right = [buf[2 + z, 3, rows, :] for z in range(CZ)]
-        w = 2
-        while len(left) > 1:
-            left = [jnp.where(lane < w, a, pltpu.roll(b, w, 1)) for a, b in zip(left[::2], left[1::2])]
-            right = [jnp.where(lane >= 128 - w, b, pltpu.roll(a, 128 - w, 1)) for a, b in zip(right[::2], right[1::2])]
-            w *= 2
-        xs[pl.ds(pl.multiple_of(8 * t, 8), 8), :] = jnp.where(lane < 64, left[0], right[0])
+        faces = jnp.zeros((8, 128), jnp.float32)
+        for z in range(CZ):
+            left = pltpu.roll(buf[2 + z, 0, rows, :], 2 * z, 1) if z else buf[2, 0, rows, :]
+            right = pltpu.roll(buf[2 + z, 3, rows, :], 66 + 2 * z, 1)
+            faces = jnp.where(pair == z, left, jnp.where(pair == 32 + z, right, faces))
+        xs[pl.ds(pl.multiple_of(8 * t, 8), 8), :] = faces
 
     for side in range(2):
         xhalo(side).start()
@@ -152,7 +151,7 @@
                     shade = jnp.abs(along) * lax.rsqrt(norm) + BIAS
                     recip = pl.reciprocal(1.0 + s)
                     bright = 1.0 - recip
-                    after = energy * jnp.exp(bright * KEXP)
+                    after = energy * jnp.exp2(bright * KEXP)
                     weight = (energy - after) * shade
                     red = weight * bright
                     state[4 * n:4 * n + 4] = [after, wsum + weight, rsum + red, bsum + red * recip]

time: 61.1 us -> 42.1 us (0.69)
  Pallas kernels: 59.7 us -> 40.6 us
    pallas_call x1, Pallas kernels: 59.7 us -> 40.6 us  [per_device(): pl.pallas_call(kernel, out_shape=jax.ShapeDtypeStruct((1, NY, NX), jnp.fl...]
where the time goes in v2:
time: 42.1 us; the launch traced here: 42 us
  Pallas kernels  40.6 us (96%)
  local copies, waits for them, and re-layouts  1.36 us (3%)
    pallas_call x1, Pallas kernels, per_device(): pl.pallas_call(kernel, out_shape=jax.ShapeDtypeStruct((1, NY, NX), jnp.fl...  40.6 us
    unnamed x3, local copies, waits for them, and re-layouts  1.36 us

profile of v2, /device:TPU:2, one launch (start us, length us, event | category | flops | bytes accessed | tf_op | source)
XLA Modules:
  0.0 42.0 jit_solution(3599736591018489786)
XLA Ops:
  0.0 0.0 copy-start
  0.0 0.7 %copy-done = s32[4]{0:T(128)S(1)} copy-done((s32[4]{0:T(128)S(1)}, s32[4]{0:T(128)}, u32[]{:S(2)}) %copy-start) | copy-done | bytes 40
  0.7 40.6 %shard_map.28 = f32[1,128,512]{2,1,0:T(8,128)S(1)} custom-call(s32[4]{0:T(128)S(1)} %copy-done, f32[32,128,512]{2,1,0:T(8,128)} %f_ref.1), custom_call_target="tpu_custom_call" | custom-call | tf_op jit(solution)/shard_map/pallas_call | solution.py:240
  41.3 0.7 %copy.4 = f32[1,128,512]{2,1,0:T(8,128)} copy(f32[1,128,512]{2,1,0:T(8,128)S(1)} %shard_map.28) | data formatting | bytes 524288
Async XLA Ops:
  0.0 0.7 %copy-start = (s32[4]{0:T(128)S(1)}, s32[4]{0:T(128)}, u32[]{:S(2)}) copy-start(s32[4]{0:T(128)} %vo_ref.1) | copy-start | bytes 52

commit v3 on v2

--- a/solution.py
+++ b/solution.py
@@ -11,7 +11,7 @@
 CZ, NY, NX = 32, 128, 512
 NB = 4
 GROUPS = 4
-STEP = 16
+STEP = 32
 TILES = ((1, 2), (0, 3))
 KEXP = -1.5 * 2.0 / 128.0 * math.log2(math.e)
 BIAS = 0.3 / 0.448
@@ -25,7 +25,6 @@
     row_to = (lax.rem(r + 1, 16), lax.rem(r + 15, 16))
     col_to = (lax.rem(c + 1, 4), lax.rem(c + 3, 4))
     lane = lax.broadcasted_iota(jnp.int32, (8, 128), 1)
-    pair = lane // 2
 
     barrier = pltpu.get_barrier_semaphore()
     others = [brick(1), brick(2), brick(3), (d, row_to[0], c), (d, row_to[1], c),
@@ -39,7 +38,7 @@
             buf.at[pl.ds(2, CZ), t, pl.ds(8 + 32 * g, 32), :], ld.at[t, g])
 
     def zhalo(p, i, side, n):
-        t, g = TILES[p][n], lax.rem(i + 1, GROUPS)
+        t, g = jnp.where(p == 0, n + 1, 3 * n), lax.rem(i + 1, GROUPS)
         src, dst, k = ((CZ - 2, 0, 1), (0, CZ + 2, 3))[side]
         return pltpu.make_async_remote_copy(
             f_ref.at[pl.ds(src, 2), pl.ds(32 * g, 32), pl.ds(128 * t, 128)],
@@ -77,14 +76,15 @@
     for t in (0, 3, 1, 2):
         for g in range(GROUPS):
             load(t, g).start()
+
     pl.semaphore_wait(barrier, len(others))
 
-    for p in range(2):
-        @pl.loop(0, GROUPS)
-        def _(i):
-            for side in range(2):
-                for n in range(2):
-                    zhalo(p, i, side, n).start()
+    @pl.loop(0, 2 * GROUPS)
+    def _(j):
+        for side in range(2):
+            for n in range(2):
+                zhalo(j // GROUPS, lax.rem(j, GROUPS), side, n).start()
+
     for side in (1, 0):
         for t in (1, 2, 0, 3):
             yhalo(t, side).start()
@@ -98,9 +98,9 @@
         rows = pl.ds(pl.multiple_of(8 + 8 * t, 8), 8)
         faces = jnp.zeros((8, 128), jnp.float32)
         for z in range(CZ):
-            left = pltpu.roll(buf[2 + z, 0, rows, :], 2 * z, 1) if z else buf[2, 0, rows, :]
-            right = pltpu.roll(buf[2 + z, 3, rows, :], 66 + 2 * z, 1)
-            faces = jnp.where(pair == z, left, jnp.where(pair == 32 + z, right, faces))
+            ends = jnp.where(lane < 64, buf[2 + z, 0, rows, :], buf[2 + z, 3, rows, :])
+            ends = pltpu.roll(ends, 4 * z, 1) if z else ends
+            faces = jnp.where(lax.rem(lane + 2, 128) // 4 == z, ends, faces)
         xs[pl.ds(pl.multiple_of(8 * t, 8), 8), :] = faces
 
     for side in range(2):
@@ -109,38 +109,28 @@
         for g in range(GROUPS):
             load(t, g).wait()
 
-    def strip(p, j, g, q):
+    def tile_of(j, n):
+        return jnp.where(j < GROUPS, n + 1, 3 * n)
+
+    def strip(j, q):
+        g = lax.rem(j + 1, GROUPS)
         row = pl.multiple_of(8 + 32 * g + 8 * q, 8)
         rows = pl.ds(row, 8)
-        tiles = TILES[p]
-        edge_rows = pl.ds(pl.multiple_of(32 * g + 8 * q, 8), 8)
-        if p == 1:
-            from_left, from_right = xr[0, edge_rows, :], xr[1, edge_rows, :]
+        tiles = tile_of(j, 0), tile_of(j, 1)
 
         def body(zz, carry):
             z0 = zz * STEP
             state = list(carry)
-            col = {t: [buf[z0 + m, t, rows, :] for m in range(STEP + 4)] for t in tiles}
-            for m in range(STEP):
-                z = z0 + m
-                for n, t in enumerate(tiles):
+            for n, t in enumerate(tiles):
+                col = [buf[z0 + m, t, rows, :] for m in range(STEP + 4)]
+                for m in range(STEP):
+                    z = z0 + m
                     energy, wsum, rsum, bsum = state[4 * n:4 * n + 4]
-                    s = col[t][m + 2]
-                    gz = 8.0 * (col[t][m + 3] - col[t][m + 1]) - (col[t][m + 4] - col[t][m])
+                    s = col[m + 2]
+                    gz = 8.0 * (col[m + 3] - col[m + 1]) - (col[m + 4] - col[m])
                     yv = lambda o: buf[z + 2, t, pl.ds(row + o, 8), :]
                     gy = 8.0 * (yv(1) - yv(-1)) - (yv(2) - yv(-2))
-                    if t == 0:
-                        prv = pltpu.roll(from_left, 62 - 2 * z, 1)
-                    elif t - 1 in tiles:
-                        prv = col[t - 1][m + 2]
-                    else:
-                        prv = buf[z + 2, t - 1, rows, :]
-                    if t == 3:
-                        nxt = pltpu.roll(from_right, lax.rem(128 - 2 * z, 128), 1)
-                    elif t + 1 in tiles:
-                        nxt = col[t + 1][m + 2]
-                    else:
-                        nxt = buf[z + 2, t + 1, rows, :]
+                    prv, nxt = buf[z + 2, lax.rem(t + 4, 5), rows, :], buf[z + 2, t + 1, rows, :]
                     xp1 = pltpu.roll(jnp.where(lane < 1, nxt, s), 127, 1)
                     xp2 = pltpu.roll(jnp.where(lane < 2, nxt, s), 126, 1)
                     xm1 = pltpu.roll(jnp.where(lane >= 127, prv, s), 1, 1)
@@ -166,30 +156,35 @@
             stage[j, q, 4 + n] = 4.0 * SCALE * bsum
             stage[j, q, 6 + n] = energy
 
-    for p in range(2):
-        if p == 1:
+    @pl.loop(0, 2 * GROUPS)
+    def _(j):
+        for side in range(2):
+            for n in range(2):
+                zhalo(j // GROUPS, lax.rem(j, GROUPS), side, n).wait()
+        for side, at in ((1, 2), (0, 3)):
+            @pl.when(j == at)
+            def _():
+                for t in range(4):
+                    yhalo(t, side).wait()
+
+        @pl.when(j == 2)
+        def _():
             for side in range(2):
                 xhalo(side).wait()
 
-        @pl.loop(0, GROUPS)
-        def _(i):
-            j, g = GROUPS * p + i, lax.rem(i + 1, GROUPS)
-            for side in range(2):
-                for n in range(2):
-                    zhalo(p, i, side, n).wait()
-            if p == 0:
-                for side, at in ((1, 2), (0, 3)):
-                    @pl.when(i == at)
-                    def _():
-                        for t in range(4):
-                            yhalo(t, side).wait()
-
-            @pl.loop(0, 4)
-            def _(q):
-                strip(p, j, g, q)
-
-            for k in range(1, NB):
-                part(j, k).start()
+            @pl.loop(0, NY // 8)
+            def _(t):
+                rows = pl.ds(pl.multiple_of(8 * t, 8), 8)
+                beyond = jnp.where(lax.rem(lane, 4) >= 2, xr[0, rows, :], xr[1, rows, :])
+                for z in range(CZ):
+                    buf[z + 2, 4, pl.ds(pl.multiple_of(8 * t + 8, 8), 8), :] = pltpu.roll(beyond, 128 - 4 * z, 1) if z else beyond
+
+        @pl.loop(0, 4)
+        def _(q):
+            strip(j, q)
+
+        for k in range(1, NB):
+            part(j, k).start()
 
     ranks = []
     for k in range(NB):
@@ -243,7 +238,7 @@
         in_specs=[pl.BlockSpec(memory_space=pltpu.SMEM), pl.BlockSpec(memory_space=pl.ANY)],
         out_specs=pl.BlockSpec(memory_space=pltpu.VMEM),
         scratch_shapes=[
-            vmem(CZ + 4, 4, NY + 16, 128),
+            vmem(CZ + 4, 5, NY + 16, 128),
             vmem(NY, 128), vmem(2, NY, 128),
             vmem(8, 4, 8, 8, 128), vmem(8, 3, 8, 8, 128),
             vmem(8, 4, 2, 8, 128), vmem(4, NY, 128),

time: 42.1 us -> 38.3 us (0.910)
  Pallas kernels: 40.6 us -> 36.9 us
    pallas_call x1, Pallas kernels: 40.6 us -> 36.9 us  [per_device(): pl.pallas_call(kernel, out_shape=jax.ShapeDtypeStruct((1, NY, NX), jnp.fl...]
where the time goes in v3:
time: 38.3 us
  Pallas kernels  36.9 us (96%)
  local copies, waits for them, and re-layouts  1.36 us (4%)
    pallas_call x1, Pallas kernels, per_device(): pl.pallas_call(kernel, out_shape=jax.ShapeDtypeStruct((1, NY, NX), jnp.fl...  36.9 us
    unnamed x3, local copies, waits for them, and re-layouts  1.36 us

profile of v3, /device:TPU:2, one launch (start us, length us, event | category | flops | bytes accessed | tf_op | source)
XLA Modules:
  0.0 38.3 jit_solution(18171987676639975881)
XLA Ops:
  0.0 0.0 copy-start
  0.0 0.7 %copy-done = s32[4]{0:T(128)S(1)} copy-done((s32[4]{0:T(128)S(1)}, s32[4]{0:T(128)}, u32[]{:S(2)}) %copy-start) | copy-done | bytes 40
  0.7 36.9 %shard_map.28 = f32[1,128,512]{2,1,0:T(8,128)S(1)} custom-call(s32[4]{0:T(128)S(1)} %copy-done, f32[32,128,512]{2,1,0:T(8,128)} %f_ref.1), custom_call_target="tpu_custom_call" | custom-call | tf_op jit(solution)/shard_map/pallas_call | solution.py:235
  37.6 0.7 %copy.4 = f32[1,128,512]{2,1,0:T(8,128)} copy(f32[1,128,512]{2,1,0:T(8,128)S(1)} %shard_map.28) | data formatting | bytes 524288
Async XLA Ops:
  0.0 0.7 %copy-start = (s32[4]{0:T(128)S(1)}, s32[4]{0:T(128)}, u32[]{:S(2)}) copy-start(s32[4]{0:T(128)} %vo_ref.1) | copy-start | bytes 52

commit v4 on v3

--- a/solution.py
+++ b/solution.py
@@ -18,8 +18,8 @@
 SCALE = 2.0 * 0.448
 
 
-def kernel(vo_ref, f_ref, o_ref, buf, xs, xr, stage, recv, fin, fbuf,
-           ld, zss, zrs, yss, yrs, xss, xrs, ass, ars, fss, frs):
+def kernel(order_ref, f_ref, o_ref, vo_ref, buf, xs, xr, stage, recv, fin, fbuf,
+           vs, ld, zss, zrs, yss, yrs, xss, xrs, ass, ars, fss, frs):
     d, r, c = lax.axis_index("depth"), lax.axis_index("row"), lax.axis_index("col")
     brick = lambda k: (lax.rem(d + k, NB), r, c)
     row_to = (lax.rem(r + 1, 16), lax.rem(r + 15, 16))
@@ -75,19 +75,18 @@
 
     for t in (0, 3, 1, 2):
         for g in range(GROUPS):
-            load(t, g).start()
-
+            load(t, g).start(priority=1)
+
+    order = pltpu.make_async_copy(order_ref, vo_ref, vs)
+    order.start()
     pl.semaphore_wait(barrier, len(others))
 
-    @pl.loop(0, 2 * GROUPS)
-    def _(j):
-        for side in range(2):
-            for n in range(2):
+    def send_zhalo(j):
+        for n in range(2):
+            for side in range(2):
                 zhalo(j // GROUPS, lax.rem(j, GROUPS), side, n).start()
 
-    for side in (1, 0):
-        for t in (1, 2, 0, 3):
-            yhalo(t, side).start()
+    pl.loop(0, 2 * GROUPS)(send_zhalo)
 
     for t in (0, 3):
         for g in range(GROUPS):
@@ -105,6 +104,9 @@
 
     for side in range(2):
         xhalo(side).start()
+    for side in (1, 0):
+        for t in (1, 2, 0, 3):
+            yhalo(t, side).start()
     for t in (1, 2):
         for g in range(GROUPS):
             load(t, g).wait()
@@ -156,36 +158,7 @@
             stage[j, q, 4 + n] = 4.0 * SCALE * bsum
             stage[j, q, 6 + n] = energy
 
-    @pl.loop(0, 2 * GROUPS)
-    def _(j):
-        for side in range(2):
-            for n in range(2):
-                zhalo(j // GROUPS, lax.rem(j, GROUPS), side, n).wait()
-        for side, at in ((1, 2), (0, 3)):
-            @pl.when(j == at)
-            def _():
-                for t in range(4):
-                    yhalo(t, side).wait()
-
-        @pl.when(j == 2)
-        def _():
-            for side in range(2):
-                xhalo(side).wait()
-
-            @pl.loop(0, NY // 8)
-            def _(t):
-                rows = pl.ds(pl.multiple_of(8 * t, 8), 8)
-                beyond = jnp.where(lax.rem(lane, 4) >= 2, xr[0, rows, :], xr[1, rows, :])
-                for z in range(CZ):
-                    buf[z + 2, 4, pl.ds(pl.multiple_of(8 * t + 8, 8), 8), :] = pltpu.roll(beyond, 128 - 4 * z, 1) if z else beyond
-
-        @pl.loop(0, 4)
-        def _(q):
-            strip(j, q)
-
-        for k in range(1, NB):
-            part(j, k).start()
-
+    order.wait()
     ranks = []
     for k in range(NB):
         b = lax.rem(d + NB - k, NB)
@@ -195,34 +168,78 @@
         ranks.append(jnp.full((8, 128), rank, jnp.int32))
     ahead = [[None if e == k else ranks[e] < ranks[k] for e in range(NB)] for k in range(NB)]
 
-    for p in range(2):
-        @pl.loop(0, GROUPS)
-        def _(i):
-            j, g = GROUPS * p + i, lax.rem(i + 1, GROUPS)
-            for k in range(1, NB):
-                part(j, k).wait()
-            for n in range(2):
-                get = lambda k, ch: stage[j, d, 2 * ch + n] if k == 0 else recv[j, k - 1, 2 * ch + n]
-                through = [get(k, 3) for k in range(NB)]
-                total = [jnp.zeros((8, 128), jnp.float32)] * 4
-                for k in range(NB):
-                    factor = jnp.ones((8, 128), jnp.float32)
-                    for e in range(NB):
-                        if e != k:
-                            factor = factor * jnp.where(ahead[k][e], through[e], 1.0)
-                    for ch in range(3):
-                        total[ch] = total[ch] + factor * get(k, ch)
-                    total[3] = total[3] + factor * (1.0 - through[k])
-                for ch in range(4):
-                    fin[j, ch, n] = total[ch]
-            for k in range(1, NB):
-                final(j, k, d).start()
-            fbuf[pl.ds(2 * p, 2), pl.ds(pl.multiple_of(32 * g + 8 * d, 8), 8), :] = fin[j, d]
+    def blend(j):
+        g = lax.rem(j + 1, GROUPS)
+        for k in range(1, NB):
+            part(j, k).wait_recv()
+        for n in range(2):
+            get = lambda k, ch: stage[j, d, 2 * ch + n] if k == 0 else recv[j, k - 1, 2 * ch + n]
+            through = [get(k, 3) for k in range(NB)]
+            total = [jnp.zeros((8, 128), jnp.float32)] * 4
+            for k in range(NB):
+                factor = jnp.ones((8, 128), jnp.float32)
+                for e in range(NB):
+                    if e != k:
+                        factor = factor * jnp.where(ahead[k][e], through[e], 1.0)
+                for ch in range(3):
+                    total[ch] = total[ch] + factor * get(k, ch)
+                total[3] = total[3] + factor * (1.0 - through[k])
+            for ch in range(4):
+                fin[j, ch, n] = total[ch]
+        for k in range(1, NB):
+            final(j, k, d).start()
+        fbuf[pl.ds(2 * (j // GROUPS), 2), pl.ds(pl.multiple_of(32 * g + 8 * d, 8), 8), :] = fin[j, d]
 
     @pl.loop(0, 2 * GROUPS)
     def _(j):
-        for k in range(1, NB):
-            final(j, k, lax.rem(d + NB - k, NB)).wait()
+        for side in range(2):
+            for n in range(2):
+                zhalo(j // GROUPS, lax.rem(j, GROUPS), side, n).wait_recv()
+        for side, at in ((1, 2), (0, 3)):
+            @pl.when(j == at)
+            def _():
+                for t in range(4):
+                    yhalo(t, side).wait_recv()
+
+        @pl.when(j == 2)
+        def _():
+            for side in range(2):
+                xhalo(side).wait_recv()
+
+            @pl.loop(0, NY // 8)
+            def _(t):
+                rows = pl.ds(pl.multiple_of(8 * t, 8), 8)
+                beyond = jnp.where(lax.rem(lane, 4) >= 2, xr[0, rows, :], xr[1, rows, :])
+                for z in range(CZ):
+                    buf[z + 2, 4, pl.ds(pl.multiple_of(8 * t + 8, 8), 8), :] = pltpu.roll(beyond, 128 - 4 * z, 1) if z else beyond
+
+        @pl.loop(0, 4)
+        def _(q):
+            strip(j, q)
+
+        for k in range(1, NB):
+            part(j, k).start()
+
+    pl.loop(0, 2 * GROUPS)(blend)
+
+    @pl.loop(0, 2 * GROUPS)
+    def _(j):
+        for k in range(1, NB):
+            part(j, k).wait_send()
+        for side in range(2):
+            for n in range(2):
+                zhalo(j // GROUPS, lax.rem(j, GROUPS), side, n).wait_send()
+
+    for side in range(2):
+        xhalo(side).wait_send()
+        for t in range(4):
+            yhalo(t, side).wait_send()
+
+    @pl.loop(0, 2 * GROUPS)
+    def _(j):
+        for k in range(1, NB):
+            final(j, k, d).wait_send()
+            final(j, k, lax.rem(d + NB - k, NB)).wait_recv()
 
     for p in range(2):
         for n in range(2):
@@ -235,19 +252,20 @@
     return pl.pallas_call(
         kernel,
         out_shape=jax.ShapeDtypeStruct((1, NY, NX), jnp.float32),
-        in_specs=[pl.BlockSpec(memory_space=pltpu.SMEM), pl.BlockSpec(memory_space=pl.ANY)],
+        in_specs=[pl.BlockSpec(memory_space=pltpu.HBM), pl.BlockSpec(memory_space=pltpu.HBM)],
         out_specs=pl.BlockSpec(memory_space=pltpu.VMEM),
         scratch_shapes=[
+            pltpu.SMEM((NB,), jnp.int32),
             vmem(CZ + 4, 5, NY + 16, 128),
             vmem(NY, 128), vmem(2, NY, 128),
             vmem(8, 4, 8, 8, 128), vmem(8, 3, 8, 8, 128),
             vmem(8, 4, 2, 8, 128), vmem(4, NY, 128),
-            dma((4, 4)), dma((2, 4, 2, 2)), dma((2, 4, 2, 2)), dma((4, 2)), dma((4, 2)),
+            dma, dma((4, 4)), dma((2, 4, 2, 2)), dma((2, 4, 2, 2)), dma((4, 2)), dma((4, 2)),
             dma((2,)), dma((2,)), dma((8, 3)), dma((8, 3)), dma((8, 3)), dma((8, 3)),
         ],
         compiler_params=pltpu.CompilerParams(
             collective_id=0, has_side_effects=True, vmem_limit_bytes=48 << 20),
-    )(view_order, field)
+    )(pltpu.with_memory_space_constraint(view_order, pltpu.HBM), field)
 
 
 def solution(mesh):

time: 38.3 us -> 37.6 us (0.982)
  local copies, waits for them, and re-layouts: 1.36 us -> 0.71 us
    unnamed x3 -> x1, local copies, waits for them, and re-layouts: 1.36 us -> 0.71 us
where the time goes in v4:
time: 37.6 us; the launch traced here: 37.5 us
  Pallas kernels  36.8 us (98%)
  local copies, waits for them, and re-layouts  0.71 us (2%)
    pallas_call x1, Pallas kernels, per_device(): pl.pallas_call(kernel, out_shape=jax.ShapeDtypeStruct((1, NY, NX), jnp.fl...  36.8 us

profile of v4, /device:TPU:2, one launch (start us, length us, event | category | flops | bytes accessed | tf_op | source)
XLA Modules:
  0.0 37.5 jit_solution(8766149965400396642)
XLA Ops:
  0.0 36.8 %shard_map.28 = f32[1,128,512]{2,1,0:T(8,128)S(1)} custom-call(s32[4]{0:T(128)} %order_ref.1, f32[32,128,512]{2,1,0:T(8,128)} %f_ref.1), custom_call_target="tpu_custom_call" | custom-call | tf_op jit(solution)/shard_map/pallas_call | solution.py:252
  36.8 0.7 %copy.4 = f32[1,128,512]{2,1,0:T(8,128)} copy(f32[1,128,512]{2,1,0:T(8,128)S(1)} %shard_map.28) | data formatting | bytes 524288

commit v5 on v4

--- a/solution.py
+++ b/solution.py
@@ -18,7 +18,7 @@
 SCALE = 2.0 * 0.448
 
 
-def kernel(order_ref, f_ref, o_ref, vo_ref, buf, xs, xr, stage, recv, fin, fbuf,
+def kernel(order_ref, f_ref, o_ref, vo_ref, answer, whole, beside, buf, xs, xr, stage, recv, fin, fbuf,
            vs, ld, zss, zrs, yss, yrs, xss, xrs, ass, ars, fss, frs):
     d, r, c = lax.axis_index("depth"), lax.axis_index("row"), lax.axis_index("col")
     brick = lambda k: (lax.rem(d + k, NB), r, c)
@@ -26,31 +26,43 @@
     col_to = (lax.rem(c + 1, 4), lax.rem(c + 3, 4))
     lane = lax.broadcasted_iota(jnp.int32, (8, 128), 1)
 
+    def pass_of(j):
+        return lax.rem(j // 2, 2)
+
+    def group_of(j):
+        return jnp.where(j < GROUPS, 1 + lax.rem(j, 2), 3 - 3 * lax.rem(j, 2))
+
+    def tile_of(j, n):
+        return jnp.where(pass_of(j) == 0, n + 1, 3 * n)
+
     barrier = pltpu.get_barrier_semaphore()
-    others = [brick(1), brick(2), brick(3), (d, row_to[0], c), (d, row_to[1], c),
-              (d, r, col_to[0]), (d, r, col_to[1])]
-    for dev in others:
-        pl.semaphore_signal(barrier, inc=1, device_id=dev, device_id_type=MESH)
+    others = [(d, row_to[0], c), (d, row_to[1], c), (d, r, col_to[0]), (d, r, col_to[1])]
+    odd = lax.rem(d, 2) == 1
+
+    @pl.when(odd)
+    def _():
+        for k in (1, 3):
+            pl.semaphore_signal(barrier, inc=1, device_id=brick(k), device_id_type=MESH)
 
     def load(t, g):
         return pltpu.make_async_copy(
             f_ref.at[:, pl.ds(32 * g, 32), pl.ds(128 * t, 128)],
             buf.at[pl.ds(2, CZ), t, pl.ds(8 + 32 * g, 32), :], ld.at[t, g])
 
-    def zhalo(p, i, side, n):
-        t, g = jnp.where(p == 0, n + 1, 3 * n), lax.rem(i + 1, GROUPS)
+    def zhalo(j, side, n):
+        t, g = tile_of(j, n), group_of(j)
         src, dst, k = ((CZ - 2, 0, 1), (0, CZ + 2, 3))[side]
         return pltpu.make_async_remote_copy(
             f_ref.at[pl.ds(src, 2), pl.ds(32 * g, 32), pl.ds(128 * t, 128)],
             buf.at[pl.ds(dst, 2), t, pl.ds(8 + 32 * g, 32), :],
-            zss.at[p, i, side, n], zrs.at[p, i, side, n],
+            zss.at[j, side, n], zrs.at[j, side, n],
             device_id=brick(k), device_id_type=MESH)
 
     def yhalo(t, side):
-        src, dst = ((NY - 8, 0), (0, NY + 8))[side]
-        return pltpu.make_async_remote_copy(
-            f_ref.at[:, pl.ds(src, 8), pl.ds(128 * t, 128)],
-            buf.at[pl.ds(2, CZ), t, pl.ds(dst, 8), :],
+        src, dst = ((NY - 2, 6), (0, NY + 8))[side]
+        return pltpu.make_async_remote_copy(
+            f_ref.at[:, pl.ds(src, 2), pl.ds(128 * t, 128)],
+            buf.at[pl.ds(2, CZ), t, pl.ds(dst, 2), :],
             yss.at[t, side], yrs.at[t, side],
             device_id=(d, row_to[side], c), device_id_type=MESH)
 
@@ -66,7 +78,7 @@
             device_id=brick(k), device_id_type=MESH)
 
     def final(j, k, owner):
-        p, g = j // GROUPS, lax.rem(j + 1, GROUPS)
+        p, g = pass_of(j), group_of(j)
         return pltpu.make_async_remote_copy(
             fin.at[j, lax.rem(d + k, NB)],
             fbuf.at[pl.ds(2 * p, 2), pl.ds(32 * g + 8 * owner, 8), :],
@@ -79,12 +91,26 @@
 
     order = pltpu.make_async_copy(order_ref, vo_ref, vs)
     order.start()
-    pl.semaphore_wait(barrier, len(others))
+
+    @pl.when(jnp.logical_not(odd))
+    def _():
+        pl.semaphore_wait(barrier, 2)
+        for k in (1, 3):
+            pl.semaphore_signal(answer, inc=1, device_id=brick(k), device_id_type=MESH)
+
+    @pl.when(odd)
+    def _():
+        pl.semaphore_wait(answer, 2)
+        for dev in others:
+            pl.semaphore_signal(barrier, inc=1, device_id=dev, device_id_type=MESH)
+        for k in (1, 3):
+            pl.semaphore_signal(whole, inc=1, device_id=brick(k), device_id_type=MESH)
+
 
     def send_zhalo(j):
         for n in range(2):
             for side in range(2):
-                zhalo(j // GROUPS, lax.rem(j, GROUPS), side, n).start()
+                zhalo(j, side, n).start()
 
     pl.loop(0, 2 * GROUPS)(send_zhalo)
 
@@ -102,20 +128,12 @@
             faces = jnp.where(lax.rem(lane + 2, 128) // 4 == z, ends, faces)
         xs[pl.ds(pl.multiple_of(8 * t, 8), 8), :] = faces
 
-    for side in range(2):
-        xhalo(side).start()
-    for side in (1, 0):
-        for t in (1, 2, 0, 3):
-            yhalo(t, side).start()
     for t in (1, 2):
         for g in range(GROUPS):
             load(t, g).wait()
 
-    def tile_of(j, n):
-        return jnp.where(j < GROUPS, n + 1, 3 * n)
-
     def strip(j, q):
-        g = lax.rem(j + 1, GROUPS)
+        g = group_of(j)
         row = pl.multiple_of(8 + 32 * g + 8 * q, 8)
         rows = pl.ds(row, 8)
         tiles = tile_of(j, 0), tile_of(j, 1)
@@ -169,7 +187,7 @@
     ahead = [[None if e == k else ranks[e] < ranks[k] for e in range(NB)] for k in range(NB)]
 
     def blend(j):
-        g = lax.rem(j + 1, GROUPS)
+        g = group_of(j)
         for k in range(1, NB):
             part(j, k).wait_recv()
         for n in range(2):
@@ -188,14 +206,36 @@
                 fin[j, ch, n] = total[ch]
         for k in range(1, NB):
             final(j, k, d).start()
-        fbuf[pl.ds(2 * (j // GROUPS), 2), pl.ds(pl.multiple_of(32 * g + 8 * d, 8), 8), :] = fin[j, d]
+        fbuf[pl.ds(2 * pass_of(j), 2), pl.ds(pl.multiple_of(32 * g + 8 * d, 8), 8), :] = fin[j, d]
+
+    @pl.when(jnp.logical_not(odd))
+    def _():
+        pl.semaphore_wait(whole, 2)
 
     @pl.loop(0, 2 * GROUPS)
     def _(j):
         for side in range(2):
             for n in range(2):
-                zhalo(j // GROUPS, lax.rem(j, GROUPS), side, n).wait_recv()
-        for side, at in ((1, 2), (0, 3)):
+                zhalo(j, side, n).wait_recv()
+        @pl.when(j == 0)
+        def _():
+            @pl.when(odd)
+            def _():
+                pl.semaphore_wait(barrier, len(others))
+                for k in (1, 3):
+                    pl.semaphore_signal(beside, inc=1, device_id=brick(k), device_id_type=MESH)
+
+            @pl.when(jnp.logical_not(odd))
+            def _():
+                pl.semaphore_wait(beside, 2)
+
+            for side in range(2):
+                xhalo(side).start()
+            for side in (1, 0):
+                for t in range(4):
+                    yhalo(t, side).start()
+
+        for side, at in ((1, 4), (0, 5)):
             @pl.when(j == at)
             def _():
                 for t in range(4):
@@ -228,7 +268,7 @@
             part(j, k).wait_send()
         for side in range(2):
             for n in range(2):
-                zhalo(j // GROUPS, lax.rem(j, GROUPS), side, n).wait_send()
+                zhalo(j, side, n).wait_send()
 
     for side in range(2):
         xhalo(side).wait_send()
@@ -256,11 +296,12 @@
         out_specs=pl.BlockSpec(memory_space=pltpu.VMEM),
         scratch_shapes=[
             pltpu.SMEM((NB,), jnp.int32),
+            pltpu.SemaphoreType.REGULAR, pltpu.SemaphoreType.REGULAR, pltpu.SemaphoreType.REGULAR,
             vmem(CZ + 4, 5, NY + 16, 128),
             vmem(NY, 128), vmem(2, NY, 128),
             vmem(8, 4, 8, 8, 128), vmem(8, 3, 8, 8, 128),
             vmem(8, 4, 2, 8, 128), vmem(4, NY, 128),
-            dma, dma((4, 4)), dma((2, 4, 2, 2)), dma((2, 4, 2, 2)), dma((4, 2)), dma((4, 2)),
+            dma, dma((4, 4)), dma((8, 2, 2)), dma((8, 2, 2)), dma((4, 2)), dma((4, 2)),
             dma((2,)), dma((2,)), dma((8, 3)), dma((8, 3)), dma((8, 3)), dma((8, 3)),
         ],
         compiler_params=pltpu.CompilerParams(

time: 37.6 us -> 37.2 us (0.989); the launches traced: 37.5 us -> 36.6 us
  Pallas kernels: 36.8 us -> 35.9 us
    pallas_call x1, Pallas kernels: 36.8 us -> 35.9 us  [per_device(): pl.pallas_call(kernel, out_shape=jax.ShapeDtypeStruct((1, NY, NX), jnp.fl...]
where the time goes in v5:
time: 37.2 us; the launch traced here: 36.6 us
  Pallas kernels  35.9 us (97%)
  local copies, waits for them, and re-layouts  0.71 us (2%)
    pallas_call x1, Pallas kernels, per_device(): pl.pallas_call(kernel, out_shape=jax.ShapeDtypeStruct((1, NY, NX), jnp.fl...  35.9 us

profile of v5, /device:TPU:2, one launch (start us, length us, event | category | flops | bytes accessed | tf_op | source)
XLA Modules:
  0.0 36.6 jit_solution(13409518594051303160)
XLA Ops:
  0.0 35.9 %shard_map.28 = f32[1,128,512]{2,1,0:T(8,128)S(1)} custom-call(s32[4]{0:T(128)} %order_ref.1, f32[32,128,512]{2,1,0:T(8,128)} %f_ref.1), custom_call_target="tpu_custom_call" | custom-call | tf_op jit(solution)/shard_map/pallas_call | solution.py:292
  35.9 0.7 %copy.4 = f32[1,128,512]{2,1,0:T(8,128)} copy(f32[1,128,512]{2,1,0:T(8,128)S(1)} %shard_map.28) | data formatting | bytes 524288

commit v6 on v5

--- a/solution.py
+++ b/solution.py
@@ -11,6 +11,7 @@
 CZ, NY, NX = 32, 128, 512
 NB = 4
 GROUPS = 4
+HOLD = 2
 STEP = 32
 TILES = ((1, 2), (0, 3))
 KEXP = -1.5 * 2.0 / 128.0 * math.log2(math.e)
@@ -38,6 +39,7 @@
     barrier = pltpu.get_barrier_semaphore()
     others = [(d, row_to[0], c), (d, row_to[1], c), (d, r, col_to[0]), (d, r, col_to[1])]
     odd = lax.rem(d, 2) == 1
+    second = lax.rem(r, 2) == 1
 
     @pl.when(odd)
     def _():
@@ -257,8 +259,22 @@
         def _(q):
             strip(j, q)
 
-        for k in range(1, NB):
-            part(j, k).start()
+        @pl.when(jnp.logical_not(second))
+        def _():
+            for k in range(1, NB):
+                part(j, k).start()
+
+        @pl.when(jnp.logical_and(second, j >= HOLD))
+        def _():
+            for k in range(1, NB):
+                part(j - HOLD, k).start()
+
+    @pl.when(second)
+    def _():
+        @pl.loop(2 * GROUPS - HOLD, 2 * GROUPS)
+        def _(j):
+            for k in range(1, NB):
+                part(j, k).start()
 
     pl.loop(0, 2 * GROUPS)(blend)
 

time: 37.2 us -> 37.8 us (1.016)
  Pallas kernels: 35.9 us -> 36.8 us
    pallas_call x1, Pallas kernels: 35.9 us -> 36.8 us  [per_device(): pl.pallas_call(kernel, out_shape=jax.ShapeDtypeStruct((1, NY, NX), jnp.fl...]
where the time goes in v6:
time: 37.8 us; the launch traced here: 37.5 us
  Pallas kernels  36.8 us (97%)
  local copies, waits for them, and re-layouts  0.71 us (2%)
    pallas_call x1, Pallas kernels, per_device(): pl.pallas_call(kernel, out_shape=jax.ShapeDtypeStruct((1, NY, NX), jnp.fl...  36.8 us

profile of v6, /device:TPU:2, one launch (start us, length us, event | category | flops | bytes accessed | tf_op | source)
XLA Modules:
  0.0 37.5 jit_solution(10381747874054773839)
XLA Ops:
  0.0 36.8 %shard_map.28 = f32[1,128,512]{2,1,0:T(8,128)S(1)} custom-call(s32[4]{0:T(128)} %order_ref.1, f32[32,128,512]{2,1,0:T(8,128)} %f_ref.1), custom_call_target="tpu_custom_call" | custom-call | tf_op jit(solution)/shard_map/pallas_call | solution.py:308
  36.8 0.7 %copy.4 = f32[1,128,512]{2,1,0:T(8,128)} copy(f32[1,128,512]{2,1,0:T(8,128)S(1)} %shard_map.28) | data formatting | bytes 524288

commit v7 on v5

--- a/solution.py
+++ b/solution.py
@@ -11,6 +11,7 @@
 CZ, NY, NX = 32, 128, 512
 NB = 4
 GROUPS = 4
+LEAD = 3
 STEP = 32
 TILES = ((1, 2), (0, 3))
 KEXP = -1.5 * 2.0 / 128.0 * math.log2(math.e)
@@ -112,7 +113,13 @@
             for side in range(2):
                 zhalo(j, side, n).start()
 
-    pl.loop(0, 2 * GROUPS)(send_zhalo)
+    second = lax.rem(r, 2) == 1
+    pl.loop(0, LEAD)(send_zhalo)
+
+    @pl.when(jnp.logical_not(second))
+    def _():
+        pl.loop(LEAD, 2 * GROUPS)(send_zhalo)
+
 
     for t in (0, 3):
         for g in range(GROUPS):
@@ -214,6 +221,10 @@
 
     @pl.loop(0, 2 * GROUPS)
     def _(j):
+        @pl.when(jnp.logical_and(second, j < 2 * GROUPS - LEAD))
+        def _():
+            send_zhalo(j + LEAD)
+
         for side in range(2):
             for n in range(2):
                 zhalo(j, side, n).wait_recv()

time: 37.2 us -> 37.2 us (level)
  no operation moved by 1% of the time
where the time goes in v7:
time: 37.2 us; the launch traced here: 36.8 us
  Pallas kernels  36.1 us (97%)
  local copies, waits for them, and re-layouts  0.71 us (2%)
    pallas_call x1, Pallas kernels, per_device(): pl.pallas_call(kernel, out_shape=jax.ShapeDtypeStruct((1, NY, NX), jnp.fl...  36.1 us

profile of v7, /device:TPU:2, one launch (start us, length us, event | category | flops | bytes accessed | tf_op | source)
XLA Modules:
  0.0 36.8 jit_solution(12073199366891868541)
XLA Ops:
  0.0 36.1 %shard_map.28 = f32[1,128,512]{2,1,0:T(8,128)S(1)} custom-call(s32[4]{0:T(128)} %order_ref.1, f32[32,128,512]{2,1,0:T(8,128)} %f_ref.1), custom_call_target="tpu_custom_call" | custom-call | tf_op jit(solution)/shard_map/pallas_call | solution.py:303
  36.1 0.7 %copy.4 = f32[1,128,512]{2,1,0:T(8,128)} copy(f32[1,128,512]{2,1,0:T(8,128)S(1)} %shard_map.28) | data formatting | bytes 524288
